TPU v7x, 32 devices: a whole 2x2x4 slice. The times are simulated.
32 devices in a mesh: brow: 8 (over z, core), bcol: 4 (over y, x).
Axes of the slice: x: 2, y: 2, z: 4, core: 2. Of those that a mesh axis runs over, the one named last changes fastest.
Arguments:
- right_side: float32 [16384, 64], P(('brow', 'bcol')), may hold values from -36 to 36
- tiles: bfloat16 [64, 1, 512, 512], P(('brow', 'bcol')), may hold values from -0.03125 to 0.03125
- row_blocks: int32 [64], P(('brow', 'bcol')), may hold values from 0 to 31, as said below
- col_blocks: int32 [64, 1], P(('brow', 'bcol')), may hold values from 0 to 31, as said below
Outputs:
- solution: float32 [16384, 64], P(('brow', 'bcol'))
- residual: float32 [16384, 64], P(('brow', 'bcol'))
Inputs may be any that keep to these rules, and one draw needn't show every extreme that they name: `row_blocks`: the 2 row blocks of one device lie in different groups, the group of block b being b % 4. `col_blocks`: the tile columns of the device at bcol index j are blocks c with c % 4 == j, different within one row slot.
All inputs are finite; a program needn't handle non-finite values.
Results may differ from a plain program's by a relative error of at most 0.0061.
Values may be sent and summed in bfloat16 or wider, within the bound.
A program may use at most 128 MiB of HBM per device.

v0:
```python
import jax
import jax.numpy as jnp
from jax import lax
from jax.sharding import PartitionSpec as P

ITERS = 3
highest = lax.Precision.HIGHEST


def solve_spd(matrix, rhs):
    factor = jnp.linalg.cholesky(matrix)
    return jax.scipy.linalg.cho_solve((factor, True), rhs)


def gram_of(left, right):
    return jnp.dot(left.T, right, precision=highest)


def right_mult(vectors, coeffs):
    return jnp.einsum("...k,kl->...l", vectors, coeffs, precision=highest)


def shards(right_side, tiles, row_blocks, col_blocks):
    groups = lax.axis_size("bcol")
    gblocks = lax.axis_size("brow")
    tile, width = right_side.shape
    slots, per_row = col_blocks.shape
    flat = tile * width
    slot_group = row_blocks % groups
    slot_place = row_blocks // groups
    col_place = col_blocks // groups
    group_ids = jnp.arange(groups, dtype=jnp.int32)
    block_ids = jnp.arange(gblocks, dtype=jnp.int32)
    matches = slot_group[:, None] == group_ids[None, :]
    wanted = jnp.sum(jnp.where(matches, slot_place[:, None], 0), axis=0)
    active = jnp.any(matches, axis=0).astype(jnp.int32)
    asked = lax.all_to_all(
        jnp.stack([wanted, active], axis=1), "bcol", split_axis=0, concat_axis=0, tiled=True
    )
    send_pick = ((asked[:, 0:1] == block_ids[None, :]) & (asked[:, 1:2] == 1)).astype(jnp.float32)
    slot_pick = matches.astype(jnp.float32)
    col_pick = (col_place.reshape(-1)[:, None] == block_ids[None, :]).astype(jnp.float32)
    own_index = lax.axis_index("brow")
    field = lax.all_gather(right_side[None], "brow", axis=0, tiled=True)

    def own(vectors):
        return lax.dynamic_index_in_dim(vectors, own_index, 0, keepdims=False)

    solution = jnp.zeros_like(field)
    residual = field
    direction = field
    rr_now = lax.psum(gram_of(own(residual), own(residual)), ("brow", "bcol"))
    for step in range(ITERS):
        stacked = direction.astype(jnp.bfloat16).reshape(gblocks, flat)
        outgoing = jnp.dot(
            send_pick.astype(jnp.bfloat16), stacked, preferred_element_type=jnp.float32
        ).astype(jnp.bfloat16)
        arrived = lax.all_to_all(outgoing, "bcol", split_axis=0, concat_axis=0, tiled=True)
        row_dir = jnp.dot(
            slot_pick.astype(jnp.bfloat16), arrived, preferred_element_type=jnp.float32
        )
        row_dir = row_dir.astype(jnp.bfloat16).reshape(slots, tile, width)
        col_dir = jnp.dot(
            col_pick.astype(jnp.bfloat16), stacked, preferred_element_type=jnp.float32
        )
        col_dir = col_dir.astype(jnp.bfloat16).reshape(slots, per_row, tile, width)
        turned = jnp.einsum("scab,sak->scbk", tiles, row_dir, preferred_element_type=jnp.float32)
        direct = jnp.einsum("scab,scbk->sak", tiles, col_dir, preferred_element_type=jnp.float32)
        local = jnp.dot(col_pick.T, turned.reshape(slots * per_row, flat), precision=highest)
        pushing = jnp.dot(slot_pick.T, direct.reshape(slots, flat), precision=highest)
        returned = lax.all_to_all(pushing, "bcol", split_axis=0, concat_axis=0, tiled=True)
        local = local + jnp.dot(send_pick.T, returned, precision=highest)
        summed = lax.psum(local.reshape(gblocks, tile, width), "brow")
        image = 3.0 * direction + summed
        curve = lax.psum(gram_of(own(direction), own(image)), ("brow", "bcol"))
        alpha = solve_spd(curve, rr_now)
        solution = solution + right_mult(direction, alpha)
        residual = residual - right_mult(image, alpha)
        if step + 1 < ITERS:
            fresh = lax.psum(gram_of(own(residual), own(residual)), ("brow", "bcol"))
            beta = solve_spd(rr_now, fresh)
            direction = residual + right_mult(direction, beta)
            rr_now = fresh
    return (own(solution), own(residual))


def solution(mesh):
    placed = (
        P(("brow", "bcol"), None),
        P(("brow", "bcol"), None, None, None),
        P(("brow", "bcol")),
        P(("brow", "bcol"), None),
    )
    return jax.shard_map(
        shards,
        mesh=mesh,
        in_specs=placed,
        out_specs=(P(("brow", "bcol"), None), P(("brow", "bcol"), None)),
        check_vma=False,
    )
```

profile of v0, /device:TPU:0, one launch (start us, length us, event | category | flops | bytes accessed | tf_op | source)
XLA Modules:
  0.0 628.7 jit_solution(16731248828745427380)
XLA Ops:
  9.4 5.2 all-to-all-start
  15.3 3.9 all-to-all-done
  19.4 15.1 %all-gather.3.cloned.1.call-done = f32[4096,64]{0,1:T(8,128)} async-done(((f32[512,64]{0,1:T(8,128)}), f32[4096,64]{0,1:T(8,128)}) %all-gather.3.cloned.1.call-update) | async-done | bytes 1048592 | tf_op jit(solution)/shard_map/all_gather | solution.py:44
  43.1 3.6 all-to-all-start.1
  52.5 4.1 all-to-all-start.2
  60.2 3.8 all-to-all-done.2
  72.3 57.7 %all-reduce.5.cloned.1.call-done = f32[8,512,64]{1,2,0:T(8,128)} async-done(((f32[8,512,64]{1,2,0:T(8,128)}), f32[8,512,64]{1,2,0:T(8,128)}) %all-reduce.5.cloned.1.call-update) | async-done | bytes 1048592 | tf_op jit(solution)/shard_map/psum | solution.py:73
  131.8 40.0 %all-reduce = (f32[64,64]{0,1:T(8,128)S(1)}, f32[64,64]{0,1:T(8,128)S(1)}) all-reduce(f32[64,64]{0,1:T(8,128)S(1)} %fusion.29, f32[64,64]{0,1:T(8,128)S(1)} %fusion.31), channel_id=1, replica_groups=mesh['brow'=8,'bcol'=4] {'brow','bcol'}, use_global_device_ids=true, to_apply=%region_6.8 | all-reduce | flops 8192 | bytes 65536 | tf_op jit(solution)/shard_map/psum | solution.py:52
  171.8 5.8 cholesky.89
  179.0 4.9 custom-call.11
  187.1 40.0 %psum.66 = f32[64,64]{0,1:T(8,128)S(1)} all-reduce(f32[64,64]{0,1:T(8,128)S(1)} %fusion.41), channel_id=1, replica_groups=mesh['brow'=8,'bcol'=4] {'brow','bcol'}, use_global_device_ids=true, to_apply=%region_7.10 | all-reduce | flops 4096 | bytes 32768 | tf_op jit(solution)/shard_map/psum | solution.py:80
  227.1 5.8 cholesky.100
  234.3 4.9 custom-call.12
  255.0 4.7 all-to-all-start.3
  270.7 4.2 all-to-all-start.4
  283.7 3.4 convolution_add_fusion.1
  287.1 3.4 reshape.125
  293.7 5.8 cholesky.122
  300.9 4.9 custom-call.14
  305.8 46.6 %all-reduce.7.cloned.1.call-done = f32[8,512,64]{1,2,0:T(8,128)} async-done(((f32[8,512,64]{1,2,0:T(8,128)}), f32[8,512,64]{1,2,0:T(8,128)}) %all-reduce.7.cloned.1.call-update) | async-done | bytes 1048592 | tf_op jit(solution)/shard_map/psum | solution.py:73
  355.1 39.8 %psum.68 = f32[64,64]{0,1:T(8,128)S(1)} all-reduce(f32[64,64]{0,1:T(8,128)S(1)} %fusion.38), channel_id=1, replica_groups=mesh['brow'=8,'bcol'=4] {'brow','bcol'}, use_global_device_ids=true, to_apply=%region_9.12 | all-reduce | flops 4096 | bytes 32768 | tf_op jit(solution)/shard_map/psum | solution.py:75
  395.0 5.8 cholesky.111
  402.2 4.9 custom-call.13
  412.2 40.0 %psum.69 = f32[64,64]{1,0:T(8,128)S(1)} all-reduce(f32[64,64]{1,0:T(8,128)S(1)} %fusion.36), channel_id=1, replica_groups=mesh['brow'=8,'bcol'=4] {'brow','bcol'}, use_global_device_ids=true, to_apply=%region_10.13 | all-reduce | flops 4096 | bytes 32768 | tf_op jit(solution)/shard_map/psum | solution.py:80
  452.7 3.6 fusion.103
  467.8 4.5 all-to-all-start.5
  482.4 4.2 all-to-all-start.6
  498.9 3.4 reshape.131
  509.6 54.4 %all-reduce.9.cloned.1.call-done = f32[8,512,64]{1,2,0:T(8,128)} async-done(((f32[8,512,64]{1,2,0:T(8,128)}), f32[8,512,64]{1,2,0:T(8,128)}) %all-reduce.9.cloned.1.call-update) | async-done | bytes 1048592 | tf_op jit(solution)/shard_map/psum | solution.py:73
  565.9 39.4 %psum.71 = f32[64,64]{0,1:T(8,128)S(1)} all-reduce(f32[64,64]{0,1:T(8,128)S(1)} %fusion.33), channel_id=1, replica_groups=mesh['brow'=8,'bcol'=4] {'brow','bcol'}, use_global_device_ids=true, to_apply=%region_12.15 | all-reduce | flops 4096 | bytes 32768 | tf_op jit(solution)/shard_map/psum | solution.py:75
  605.4 5.8 cholesky.133
  612.6 4.9 custom-call.15
  (169 shorter events, 135.3 us)
Async XLA Ops:
  7.2 39.7 %copy-start = (bf16[2,1,512,512]{3,2,1,0:T(8,128)(2,1)S(1)}, bf16[2,1,512,512]{3,2,1,0:T(8,128)(2,1)}, u32[]{:S(2)}) copy-start(bf16[2,1,512,512]{3,2,1,0:T(8,128)(2,1)} %param.8) | copy-start | bytes 3145732
  7.2 27.3 %all-gather.3.cloned.1.call-start = ((), (), s32[]{:S(2)}) async-start(), calls=%async_computation.10 | async-start | bytes 1179648 | tf_op jit(solution)/shard_map/all_gather | solution.py:44
  9.4 9.7 %all-to-all-start = ((s32[4,1,2]{2,1,0:T(1,128)}), s32[4,1,2]{2,1,0:T(1,128)S(1)}, u32[]{:S(2)}, u32[]{:S(2)}) async-start(s32[4,1,2]{2,1,0:T(1,128)} %copy.164), calls=%async_computation | async-start | bytes 4096 | tf_op jit(solution)/shard_map/all_to_all | solution.py:37
  43.1 9.4 %all-to-all-start.1 = ((bf16[4,2,16384]{2,1,0:T(2,128)(2,1)}), bf16[4,2,16384]{2,1,0:T(2,128)(2,1)S(1)}, u32[]{:S(2)}, u32[]{:S(2)}) async-start(bf16[4,2,16384]{2,1,0:T(2,128)(2,1)} %reshape.142), calls=%async_computation.1 | async-start | bytes 524288 | tf_op jit(solution)/shard_map/all_to_all | solution.py:58
  52.5 11.6 %all-to-all-start.2 = ((f32[4,1,32768]{2,1,0:T(1,128)}), f32[4,1,32768]{2,1,0:T(1,128)}, u32[]{:S(2)}, u32[]{:S(2)}) async-start(f32[4,1,32768]{2,1,0:T(1,128)} %copy.172), calls=%async_computation.2 | async-start | bytes 1048576 | tf_op jit(solution)/shard_map/all_to_all | solution.py:71
  56.6 73.3 %all-reduce.5.cloned.1.call-start = ((), (), s32[]{:S(2)}) async-start(), calls=%async_computation.7 | async-start | bytes 2097152 | tf_op jit(solution)/shard_map/psum | solution.py:73
  68.6 61.3 %copy-start.1 = (f32[4096,64]{0,1:T(8,128)S(1)}, f32[4096,64]{0,1:T(8,128)}, u32[]{:S(2)}) copy-start(f32[4096,64]{0,1:T(8,128)} %all-gather.3.cloned.1.call-done) | copy-start | bytes 3145732
  129.9 54.6 %copy-start.6 = (f32[8,512,64]{1,2,0:T(8,128)S(1)}, f32[8,512,64]{1,2,0:T(8,128)}, u32[]{:S(2)}) copy-start(f32[8,512,64]{1,2,0:T(8,128)} %all-reduce.5.cloned.1.call-done) | copy-start | bytes 3145732
  184.5 1.3 copy-start.7
  185.8 1.0 copy-start.2
  255.0 15.7 %all-to-all-start.3 = ((bf16[4,2,16384]{2,1,0:T(2,128)(2,1)}), bf16[4,2,16384]{2,1,0:T(2,128)(2,1)S(1)}, u32[]{:S(2)}, u32[]{:S(2)}) async-start(bf16[4,2,16384]{2,1,0:T(2,128)(2,1)} %reshape.144), calls=%async_computation.3 | async-start | bytes 524288 | tf_op jit(solution)/shard_map/all_to_all | solution.py:58
  270.7 13.0 %all-to-all-start.4 = ((f32[4,1,32768]{2,1,0:T(1,128)}), f32[4,1,32768]{2,1,0:T(1,128)}, u32[]{:S(2)}, u32[]{:S(2)}) async-start(f32[4,1,32768]{2,1,0:T(1,128)} %copy.191), calls=%async_computation.4 | async-start | bytes 1048576 | tf_op jit(solution)/shard_map/all_to_all | solution.py:71
  274.9 77.4 %all-reduce.7.cloned.1.call-start = ((), (), s32[]{:S(2)}) async-start(), calls=%async_computation.8 | async-start | bytes 2097152 | tf_op jit(solution)/shard_map/psum | solution.py:73
  353.8 1.0 copy-start.5
  407.6 0.6 copy-start.9
  410.9 1.0 copy-start.4
  452.2 6.4 %copy-start.11 = (f32[64,64]{1,0:T(8,128)}, f32[64,64]{1,0:T(8,128)S(1)}, u32[]{:S(2)}) copy-start(f32[64,64]{1,0:T(8,128)S(1)} %psum.69) | copy-start | bytes 49156
  467.8 14.5 %all-to-all-start.5 = ((bf16[4,2,16384]{2,1,0:T(2,128)(2,1)}), bf16[4,2,16384]{2,1,0:T(2,128)(2,1)S(1)}, u32[]{:S(2)}, u32[]{:S(2)}) async-start(bf16[4,2,16384]{2,1,0:T(2,128)(2,1)} %reshape.146), calls=%async_computation.5 | async-start | bytes 524288 | tf_op jit(solution)/shard_map/all_to_all | solution.py:58
  482.4 13.2 %all-to-all-start.6 = ((f32[4,1,32768]{2,1,0:T(1,128)}), f32[4,1,32768]{2,1,0:T(1,128)}, u32[]{:S(2)}, u32[]{:S(2)}) async-start(f32[4,1,32768]{2,1,0:T(1,128)} %copy.205), calls=%async_computation.6 | async-start | bytes 1048576 | tf_op jit(solution)/shard_map/all_to_all | solution.py:71
  486.6 77.5 %all-reduce.9.cloned.1.call-start = ((), (), s32[]{:S(2)}) async-start(), calls=%async_computation.9 | async-start | bytes 2097152 | tf_op jit(solution)/shard_map/psum | solution.py:73
  502.3 3.2 copy-start.8
  505.4 2.1 copy-start.10
  507.5 56.6 %copy-start.3 = (f32[8,512,64]{1,2,0:T(8,128)S(1)}, f32[8,512,64]{1,2,0:T(8,128)}, u32[]{:S(2)}) copy-start(f32[8,512,64]{1,2,0:T(8,128)} %get-tuple-element.11) | copy-start | bytes 3145732
  509.6 107.9 %copy-start.12 = (f32[64,64]{1,0:T(8,128)S(1)}, f32[64,64]{1,0:T(8,128)}, u32[]{:S(2)}) copy-start(f32[64,64]{1,0:T(8,128)} %copy-done.11) | copy-start | bytes 49156
Sparse Core Ops, SparseCore 0:
  9.6 24.7 all-gather.2
  72.0 57.8 all-reduce.4
  293.8 58.5 all-reduce.6
  505.6 58.4 all-reduce.8
where the time goes:
time: 639 us; the launch traced here: 629 us
  blocking collectives  199 us (31%)
  waiting for transfers between devices  185 us (29%)
  other arithmetic  73 us (11%)
  local copies, waits for them, and re-layouts  67.7 us (11%)
  matrix products  58.6 us (9%)
  starting transfers between devices  30.7 us (5%)
  between operations  14.6 us (2%)
    psum x3, waiting for transfers between devices, shards(): summed = lax.psum(local.reshape(gblocks, tile, width), 'brow')  159 us
    psum x2, blocking collectives, shards(): fresh = lax.psum(gram_of(own(residual), own(residual)), ('brow', 'bcol'))  80 us
    psum x2, blocking collectives, shards(): curve = lax.psum(gram_of(own(direction), own(image)), ('brow', 'bcol'))  79.3 us
    psum x1, blocking collectives, shards(): rr_now = lax.psum(gram_of(own(residual), own(residual)), ('brow', 'bcol'))  40 us
    another operation x15, other arithmetic, solve_spd(): factor = jnp.linalg.cholesky(matrix)  32.6 us
    another operation x10, other arithmetic, solve_spd(): return jax.scipy.linalg.cho_solve((factor, True), rhs)  27.7 us
    reshape x6, local copies, waits for them, and re-layouts, shards(): summed = lax.psum(local.reshape(gblocks, tile, width), 'brow')  18.6 us
    dot_general x8, matrix products, right_mult(): return jnp.einsum('...k,kl->...l', vectors, coeffs, precision=highest)  17 us
  transfers between devices with their start and end apart: 11, of which 7 were waited for; matrix products, arithmetic and copies ran while one was open for 10% of the time, Pallas kernels for 0%

commit v1 on v0

--- a/solution.py
+++ b/solution.py
@@ -49,7 +49,7 @@
     solution = jnp.zeros_like(field)
     residual = field
     direction = field
-    rr_now = lax.psum(gram_of(own(residual), own(residual)), ("brow", "bcol"))
+    rr_now = lax.psum(lax.psum(gram_of(own(residual), own(residual)), "bcol"), "brow")
     for step in range(ITERS):
         stacked = direction.astype(jnp.bfloat16).reshape(gblocks, flat)
         outgoing = jnp.dot(

time: 639 us -> 662 us (1.036)
  blocking collectives: 199 us -> 242 us
  waiting for transfers between devices: 185 us -> 169 us
    psum x2 -> x3, blocking collectives: 79.3 us -> 118 us  [shards(): curve = lax.psum(gram_of(own(direction), own(image)), ('brow', 'bcol'))]
    psum x3, waiting for transfers between devices: 159 us -> 146 us  [shards(): summed = lax.psum(local.reshape(gblocks, tile, width), 'brow')]
    psum x1 -> x2, blocking collectives: 40 us -> 42.7 us  [the longest x1 25.9 us: shards(): lax.psum(lax.psum(gram_of(own(residual), own(residual)), 'bcol'), 'brow')]
  transfers between devices with their start and end apart: 11 -> 11, of which waited for: 7 -> 6; matrix products, arithmetic and copies ran while one was open for 10% -> 12% of each run, Pallas kernels for 0% -> 0%
where the time goes in v1:
time: 662 us; the launch traced here: 654 us
  blocking collectives  242 us (37%)
  waiting for transfers between devices  169 us (26%)
  other arithmetic  73 us (11%)
  local copies, waits for them, and re-layouts  67.7 us (10%)
  matrix products  57.2 us (9%)
  starting transfers between devices  30.9 us (5%)
  between operations  14.6 us (2%)
    psum x3, waiting for transfers between devices, shards(): summed = lax.psum(local.reshape(gblocks, tile, width), 'brow')  146 us
    psum x3, blocking collectives, shards(): curve = lax.psum(gram_of(own(direction), own(image)), ('brow', 'bcol'))  118 us
    psum x2, blocking collectives, shards(): fresh = lax.psum(gram_of(own(residual), own(residual)), ('brow', 'bcol'))  80.8 us
    another operation x15, other arithmetic, solve_spd(): factor = jnp.linalg.cholesky(matrix)  32.6 us
    another operation x10, other arithmetic, solve_spd(): return jax.scipy.linalg.cho_solve((factor, True), rhs)  27.7 us
    psum x1, blocking collectives, shards(): lax.psum(lax.psum(gram_of(own(residual), own(residual)), 'bcol'), 'brow')  25.9 us
    reshape x6, local copies, waits for them, and re-layouts, shards(): summed = lax.psum(local.reshape(gblocks, tile, width), 'brow')  18.6 us
    dot_general x8, matrix products, right_mult(): return jnp.einsum('...k,kl->...l', vectors, coeffs, precision=highest)  17 us
  transfers between devices with their start and end apart: 11, of which 6 were waited for; matrix products, arithmetic and copies ran while one was open for 12% of the time, Pallas kernels for 0%

profile of v1, /device:TPU:0, one launch (start us, length us, event | category | flops | bytes accessed | tf_op | source)
XLA Modules:
  0.0 654.5 jit_solution(7634322580162986920)
XLA Ops:
  9.4 5.2 all-to-all-start
  15.3 3.9 all-to-all-done
  19.4 15.1 %all-gather.3.cloned.1.call-done = f32[4096,64]{0,1:T(8,128)} async-done(((f32[512,64]{0,1:T(8,128)}), f32[4096,64]{0,1:T(8,128)}) %all-gather.3.cloned.1.call-update) | async-done | bytes 1048592 | tf_op jit(solution)/shard_map/all_gather | solution.py:44
  43.1 3.6 all-to-all-start.1
  47.7 16.8 %psum.72 = f32[64,64]{0,1:T(8,128)S(1)} all-reduce(f32[64,64]{0,1:T(8,128)S(1)} %fusion.29), channel_id=1, replica_groups=mesh['brow'=8,'bcol'=4] {'bcol'}, use_global_device_ids=true, to_apply=%region_6.8 | all-reduce | flops 4096 | bytes 32768 | tf_op jit(solution)/shard_map/psum | solution.py:52
  64.5 25.9 %psum.73 = f32[64,64]{0,1:T(8,128)S(1)} all-reduce(f32[64,64]{0,1:T(8,128)S(1)} %psum.72), channel_id=1, replica_groups=mesh['brow'=8,'bcol'=4] {'brow'}, use_global_device_ids=true, to_apply=%region_7.9 | all-reduce | flops 4096 | bytes 32768 | tf_op jit(solution)/shard_map/psum | solution.py:52
  93.2 4.1 all-to-all-start.2
  100.1 3.9 all-to-all-done.2
  111.4 5.8 cholesky.100
  118.6 4.9 custom-call.12
  123.5 44.3 %all-reduce.4.cloned.1.call-done = f32[8,512,64]{1,2,0:T(8,128)} async-done(((f32[8,512,64]{1,2,0:T(8,128)}), f32[8,512,64]{1,2,0:T(8,128)}) %all-reduce.4.cloned.1.call-update) | async-done | bytes 1048592 | tf_op jit(solution)/shard_map/psum | solution.py:73
  169.6 39.5 %psum.71 = f32[64,64]{0,1:T(8,128)S(1)} all-reduce(f32[64,64]{0,1:T(8,128)S(1)} %fusion.31), channel_id=1, replica_groups=mesh['brow'=8,'bcol'=4] {'brow','bcol'}, use_global_device_ids=true, to_apply=%region_3.4 | all-reduce | flops 4096 | bytes 32768 | tf_op jit(solution)/shard_map/psum | solution.py:75
  209.2 5.8 cholesky.89
  216.4 4.9 custom-call.11
  224.4 40.3 %psum.74 = f32[64,64]{0,1:T(8,128)S(1)} all-reduce(f32[64,64]{0,1:T(8,128)S(1)} %fusion.41), channel_id=1, replica_groups=mesh['brow'=8,'bcol'=4] {'brow','bcol'}, use_global_device_ids=true, to_apply=%region_8.11 | all-reduce | flops 4096 | bytes 32768 | tf_op jit(solution)/shard_map/psum | solution.py:80
  280.4 4.5 all-to-all-start.3
  295.9 4.2 all-to-all-start.4
  312.5 3.4 reshape.125
  319.1 5.8 cholesky.122
  326.3 4.9 custom-call.14
  331.2 46.8 %all-reduce.6.cloned.1.call-done = f32[8,512,64]{1,2,0:T(8,128)} async-done(((f32[8,512,64]{1,2,0:T(8,128)}), f32[8,512,64]{1,2,0:T(8,128)}) %all-reduce.6.cloned.1.call-update) | async-done | bytes 1048592 | tf_op jit(solution)/shard_map/psum | solution.py:73
  380.7 39.5 %psum.76 = f32[64,64]{0,1:T(8,128)S(1)} all-reduce(f32[64,64]{0,1:T(8,128)S(1)} %fusion.38), channel_id=1, replica_groups=mesh['brow'=8,'bcol'=4] {'brow','bcol'}, use_global_device_ids=true, to_apply=%region_10.13 | all-reduce | flops 4096 | bytes 32768 | tf_op jit(solution)/shard_map/psum | solution.py:75
  420.3 5.8 cholesky.111
  427.4 4.9 custom-call.13
  437.4 40.5 %psum.77 = f32[64,64]{1,0:T(8,128)S(1)} all-reduce(f32[64,64]{1,0:T(8,128)S(1)} %fusion.36), channel_id=1, replica_groups=mesh['brow'=8,'bcol'=4] {'brow','bcol'}, use_global_device_ids=true, to_apply=%region_11.14 | all-reduce | flops 4096 | bytes 32768 | tf_op jit(solution)/shard_map/psum | solution.py:80
  478.4 3.6 fusion.103
  493.6 4.5 all-to-all-start.5
  508.1 4.2 all-to-all-start.6
  535.4 54.5 %all-reduce.8.cloned.1.call-done = f32[8,512,64]{1,2,0:T(8,128)} async-done(((f32[8,512,64]{1,2,0:T(8,128)}), f32[8,512,64]{1,2,0:T(8,128)}) %all-reduce.8.cloned.1.call-update) | async-done | bytes 1048592 | tf_op jit(solution)/shard_map/psum | solution.py:73
  591.6 39.5 %psum.79 = f32[64,64]{0,1:T(8,128)S(1)} all-reduce(f32[64,64]{0,1:T(8,128)S(1)} %fusion.33), channel_id=1, replica_groups=mesh['brow'=8,'bcol'=4] {'brow','bcol'}, use_global_device_ids=true, to_apply=%region_13.16 | all-reduce | flops 4096 | bytes 32768 | tf_op jit(solution)/shard_map/psum | solution.py:75
  631.2 5.8 cholesky.133
  638.4 4.9 custom-call.15
  (171 shorter events, 138.6 us)
Async XLA Ops:
  7.2 39.9 %copy-start = (bf16[2,1,512,512]{3,2,1,0:T(8,128)(2,1)S(1)}, bf16[2,1,512,512]{3,2,1,0:T(8,128)(2,1)}, u32[]{:S(2)}) copy-start(bf16[2,1,512,512]{3,2,1,0:T(8,128)(2,1)} %param.8) | copy-start | bytes 3145732
  7.2 27.3 %all-gather.3.cloned.1.call-start = ((), (), s32[]{:S(2)}) async-start(), calls=%async_computation.10 | async-start | bytes 1179648 | tf_op jit(solution)/shard_map/all_gather | solution.py:44
  9.4 9.7 %all-to-all-start = ((s32[4,1,2]{2,1,0:T(1,128)}), s32[4,1,2]{2,1,0:T(1,128)S(1)}, u32[]{:S(2)}, u32[]{:S(2)}) async-start(s32[4,1,2]{2,1,0:T(1,128)} %copy.164), calls=%async_computation | async-start | bytes 4096 | tf_op jit(solution)/shard_map/all_to_all | solution.py:37
  43.1 50.1 %all-to-all-start.1 = ((bf16[4,2,16384]{2,1,0:T(2,128)(2,1)}), bf16[4,2,16384]{2,1,0:T(2,128)(2,1)S(1)}, u32[]{:S(2)}, u32[]{:S(2)}) async-start(bf16[4,2,16384]{2,1,0:T(2,128)(2,1)} %reshape.142), calls=%async_computation.1 | async-start | bytes 524288 | tf_op jit(solution)/shard_map/all_to_all | solution.py:58
  93.2 10.8 %all-to-all-start.2 = ((f32[4,1,32768]{2,1,0:T(1,128)}), f32[4,1,32768]{2,1,0:T(1,128)}, u32[]{:S(2)}, u32[]{:S(2)}) async-start(f32[4,1,32768]{2,1,0:T(1,128)} %copy.172), calls=%async_computation.2 | async-start | bytes 1048576 | tf_op jit(solution)/shard_map/all_to_all | solution.py:71
  97.3 70.5 %all-reduce.4.cloned.1.call-start = ((), (), s32[]{:S(2)}) async-start(), calls=%async_computation.7 | async-start | bytes 2097152 | tf_op jit(solution)/shard_map/psum | solution.py:73
  108.2 59.7 %copy-start.1 = (f32[4096,64]{0,1:T(8,128)S(1)}, f32[4096,64]{0,1:T(8,128)}, u32[]{:S(2)}) copy-start(f32[4096,64]{0,1:T(8,128)} %all-gather.3.cloned.1.call-done) | copy-start | bytes 3145732
  167.8 54.0 %copy-start.6 = (f32[8,512,64]{1,2,0:T(8,128)S(1)}, f32[8,512,64]{1,2,0:T(8,128)}, u32[]{:S(2)}) copy-start(f32[8,512,64]{1,2,0:T(8,128)} %all-reduce.4.cloned.1.call-done) | copy-start | bytes 3145732
  221.8 1.3 copy-start.7
  223.1 1.0 copy-start.2
  280.4 15.5 %all-to-all-start.3 = ((bf16[4,2,16384]{2,1,0:T(2,128)(2,1)}), bf16[4,2,16384]{2,1,0:T(2,128)(2,1)S(1)}, u32[]{:S(2)}, u32[]{:S(2)}) async-start(bf16[4,2,16384]{2,1,0:T(2,128)(2,1)} %reshape.144), calls=%async_computation.3 | async-start | bytes 524288 | tf_op jit(solution)/shard_map/all_to_all | solution.py:58
  295.9 13.2 %all-to-all-start.4 = ((f32[4,1,32768]{2,1,0:T(1,128)}), f32[4,1,32768]{2,1,0:T(1,128)}, u32[]{:S(2)}, u32[]{:S(2)}) async-start(f32[4,1,32768]{2,1,0:T(1,128)} %copy.191), calls=%async_computation.4 | async-start | bytes 1048576 | tf_op jit(solution)/shard_map/all_to_all | solution.py:71
  300.1 77.9 %all-reduce.6.cloned.1.call-start = ((), (), s32[]{:S(2)}) async-start(), calls=%async_computation.8 | async-start | bytes 2097152 | tf_op jit(solution)/shard_map/psum | solution.py:73
  379.4 1.0 copy-start.5
  432.8 0.6 copy-start.9
  436.2 1.0 copy-start.4
  477.9 6.4 copy-start.11
  493.6 14.5 %all-to-all-start.5 = ((bf16[4,2,16384]{2,1,0:T(2,128)(2,1)}), bf16[4,2,16384]{2,1,0:T(2,128)(2,1)S(1)}, u32[]{:S(2)}, u32[]{:S(2)}) async-start(bf16[4,2,16384]{2,1,0:T(2,128)(2,1)} %reshape.146), calls=%async_computation.5 | async-start | bytes 524288 | tf_op jit(solution)/shard_map/all_to_all | solution.py:58
  508.1 13.2 %all-to-all-start.6 = ((f32[4,1,32768]{2,1,0:T(1,128)}), f32[4,1,32768]{2,1,0:T(1,128)}, u32[]{:S(2)}, u32[]{:S(2)}) async-start(f32[4,1,32768]{2,1,0:T(1,128)} %copy.205), calls=%async_computation.6 | async-start | bytes 1048576 | tf_op jit(solution)/shard_map/all_to_all | solution.py:71
  512.3 77.6 %all-reduce.8.cloned.1.call-start = ((), (), s32[]{:S(2)}) async-start(), calls=%async_computation.9 | async-start | bytes 2097152 | tf_op jit(solution)/shard_map/psum | solution.py:73
  528.0 3.2 copy-start.8
  531.2 2.1 copy-start.10
  533.3 56.6 %copy-start.3 = (f32[8,512,64]{1,2,0:T(8,128)S(1)}, f32[8,512,64]{1,2,0:T(8,128)}, u32[]{:S(2)}) copy-start(f32[8,512,64]{1,2,0:T(8,128)} %get-tuple-element.9) | copy-start | bytes 3145732
  535.4 107.9 %copy-start.12 = (f32[64,64]{1,0:T(8,128)S(1)}, f32[64,64]{1,0:T(8,128)}, u32[]{:S(2)}) copy-start(f32[64,64]{1,0:T(8,128)} %copy-done.11) | copy-start | bytes 49156
Sparse Core Ops, SparseCore 0:
  9.6 24.7 all-gather.2
  111.6 56.2 all-reduce.3
  319.2 58.6 all-reduce.5
  531.3 58.4 all-reduce.7
